TPU v7x, 256 devices: a whole 4x4x8 slice. The times are simulated.
256 devices in a mesh: section: 8 (over y, z_lo), replica: 32 (over z_hi, x, core).
Axes of the slice: x: 4, y: 4, z: 8 (z_hi: 4, z_lo: 2; z = z_hi * 2 + z_lo), core: 2. Of those that a mesh axis runs over, the one named last changes fastest.
Arguments:
- section_inputs: bfloat16 [8, 11264, 1280], P('section', 'replica'), may hold values from -6 to 6
- in_weight: bfloat16 [8, 1280, 2560], P('section', 'replica'), may hold values from -0.15625 to 0.15625
- out_weight: bfloat16 [8, 2560, 1280], P('section', 'replica'), may hold values from -0.125 to 0.125
- projection: bfloat16 [1280, 512], replicated, may hold values from -0.15625 to 0.15625
- text_embed: bfloat16 [256, 512], P('replica'), may hold values from -6 to 6
- pair_label: int32 [128, 2], P('replica'), may hold values from 0 to 1, each once within a row
- pool_group: int32 [32], replicated, may hold values from 0 to 7
Outputs:
- input_grad: bfloat16 [8, 11264, 1280], P('section', 'replica')
- in_weight_grad: float32 [8, 1280, 2560], P('section', 'replica')
- out_weight_grad: float32 [8, 2560, 1280], P('section', 'replica')
Inputs may be any that keep to these rules, and one draw needn't show every extreme that they name: Each row of pair_label is a permutation of the 2 slots.
All inputs are finite; a program needn't handle non-finite values.
Results may differ from a plain program's by a relative error of at most 0.04.
Values may be sent and summed in bfloat16 or wider, within the bound.
No kernel may reach another device: no remote copies, remote signals or barrier semaphores. Data moves between devices by JAX's collectives and lax.ppermute only.
A program may use at most 128 MiB of HBM per device.

v0:
```python
import jax
import jax.numpy as jnp
from jax import lax
from jax.sharding import PartitionSpec as P

MICRO = 4
FRAMES = 44


eps_norm = 1e-05
eps_unit = 1e-06
inv_temp = 1.0 / 0.07
grad_scale = 256.0
sqrt_half = 0.7071067811865476
inv_sqrt_two_pi = 0.3989422804014327


def shifted(block, axis, distance):
    devices = range(lax.axis_size(axis))
    route = [(i - distance, i) for i in devices if i - distance in devices]
    return lax.ppermute(block, axis, route)


def layer_norm(values):
    average = jnp.mean(values, axis=-1, keepdims=True)
    centred = values - average
    inv_std = lax.rsqrt(jnp.mean(centred * centred, axis=-1, keepdims=True) + eps_norm)
    return (centred * inv_std, inv_std)


def norm_backward(upstream, centred, inv_std):
    first = jnp.mean(upstream, axis=-1, keepdims=True)
    second = jnp.mean(upstream * centred, axis=-1, keepdims=True)
    return inv_std * (upstream - first - centred * second)


def gelu_exact(values):
    return 0.5 * values * (1.0 + lax.erf(values * sqrt_half))


def gelu_slope(values):
    return (
        0.5 * (1.0 + lax.erf(values * sqrt_half))
        + values * jnp.exp(-0.5 * values * values) * inv_sqrt_two_pi
    )


def block_front(inputs, first_weight):
    centred, inv_std = layer_norm(inputs.astype(jnp.float32))
    normed = centred.astype(jnp.bfloat16)
    preact = jnp.dot(normed, first_weight, preferred_element_type=jnp.float32)
    hidden = gelu_exact(preact).astype(jnp.bfloat16)
    return (normed, preact, hidden)


def block_output(inputs, hidden, second_weight):
    return inputs.astype(jnp.float32) + jnp.dot(
        hidden, second_weight, preferred_element_type=jnp.float32
    )


def block_backward(out_grad, inputs, preact, first_weight, second_weight):
    act_grad = lax.dot_general(
        out_grad, second_weight, (((1,), (1,)), ((), ())), preferred_element_type=jnp.float32
    )
    pre_grad = (act_grad * gelu_slope(preact)).astype(jnp.bfloat16)
    normed_grad = lax.dot_general(
        pre_grad, first_weight, (((1,), (1,)), ((), ())), preferred_element_type=jnp.float32
    )
    centred, inv_std = layer_norm(inputs.astype(jnp.float32))
    in_grad = (out_grad.astype(jnp.float32) + norm_backward(normed_grad, centred, inv_std)).astype(
        jnp.bfloat16
    )
    return (in_grad, pre_grad)


def audio_embed(block_out, projection, frames):
    centred, inv_std = layer_norm(block_out)
    width = centred.shape[1]
    pooled = jnp.mean(centred.reshape(-1, frames, width), axis=1).astype(jnp.bfloat16)
    embedded = jnp.dot(pooled, projection, preferred_element_type=jnp.float32)
    inv_norm = lax.rsqrt(jnp.sum(embedded * embedded, axis=-1, keepdims=True) + eps_unit)
    return (embedded * inv_norm, inv_norm, centred, inv_std)


def embed_backward(audio_grad, audio_unit, inv_norm, projection, centred, inv_std, frames):
    emb_grad = (
        audio_grad - audio_unit * jnp.sum(audio_unit * audio_grad, axis=-1, keepdims=True)
    ) * inv_norm
    pooled_grad = jnp.dot(
        emb_grad, projection.astype(jnp.float32).T, precision=lax.Precision.HIGHEST
    )
    row_grad = jnp.repeat(pooled_grad / frames, frames, axis=0)
    return norm_backward(row_grad, centred, inv_std).astype(jnp.bfloat16)


def paired_texts(text_embed, pair_label):
    texts = text_embed.astype(jnp.float32)
    unit_text = texts * lax.rsqrt(jnp.sum(texts * texts, axis=-1, keepdims=True) + eps_unit)
    slots = pair_label.shape[1]
    unit_text = unit_text.reshape(-1, slots, unit_text.shape[1])
    chooser = (pair_label[:, :, None] == jnp.arange(slots, dtype=jnp.int32)[None, None, :]).astype(
        jnp.float32
    )
    chosen = jnp.einsum("mcj,mje->mce", chooser, unit_text, precision=lax.Precision.HIGHEST)
    return chosen.reshape(-1, chosen.shape[2])


def pair_weights(audio_all, text_all, groups):
    scores = jnp.dot(audio_all, text_all.T, precision=lax.Precision.HIGHEST) * inv_temp
    same_group = (groups[:, None] == groups[None, :]).astype(jnp.float32)
    weighted = same_group * jnp.exp(scores)
    by_rows = weighted / jnp.sum(weighted, axis=1, keepdims=True)
    by_cols = weighted / jnp.sum(weighted, axis=0, keepdims=True)
    return by_rows + by_cols


def take_micro(stacked, which_micro):
    return lax.dynamic_index_in_dim(stacked, which_micro, 0, keepdims=False)


def store_micro(stacked, update, which_micro):
    return lax.dynamic_update_index_in_dim(stacked, update, which_micro, 0)


def local(section_inputs, in_weight, out_weight, projection, text_embed, pair_label, pool_group):
    inputs = section_inputs[0]
    row_count = inputs.shape[0]
    per_micro = row_count // MICRO
    first_weight, second_weight = (
        lax.all_gather(in_weight[0], "replica", axis=0, tiled=True),
        lax.all_gather(out_weight[0], "replica", axis=0, tiled=True),
    )
    normed, preact, hidden = block_front(inputs, first_weight)
    block_out = block_output(inputs, hidden, second_weight)
    audio_unit, inv_norm, centred, inv_std = audio_embed(block_out, projection, FRAMES)
    local_text = paired_texts(text_embed, pair_label)
    audio_all, text_all = (
        lax.all_gather(audio_unit.astype(jnp.bfloat16), "replica", axis=0, tiled=True).astype(
            audio_unit.dtype
        ),
        lax.all_gather(local_text.astype(jnp.bfloat16), "replica", axis=0, tiled=True).astype(
            local_text.dtype
        ),
    )
    clip_count = audio_unit.shape[0]
    first_clip = lax.axis_index("replica") * clip_count
    groups = jnp.repeat(pool_group, clip_count)
    weights = pair_weights(audio_all, text_all, groups)
    own_weights = lax.dynamic_slice_in_dim(weights, first_clip, clip_count, 0)
    targets = (
        jnp.arange(audio_all.shape[0], dtype=jnp.int32)[None, :]
        == first_clip + jnp.arange(clip_count, dtype=jnp.int32)[:, None]
    ).astype(jnp.float32)
    coeffs = grad_scale * (own_weights - 2.0 * targets)
    audio_grad = jnp.dot(coeffs, text_all, precision=lax.Precision.HIGHEST) * inv_temp
    last_grad = embed_backward(
        audio_grad, audio_unit, inv_norm, projection, centred, inv_std, FRAMES
    )
    section_count = lax.axis_size("section")
    section_id = lax.axis_index("section")
    is_last = section_id == section_count - 1
    width = inputs.shape[1]
    inputs_micro = inputs.reshape(MICRO, per_micro, width)
    preact_micro = preact.reshape(MICRO, per_micro, preact.shape[1])
    last_micro = last_grad.reshape(MICRO, per_micro, width)

    def tick(tick_id, state_tuple):
        incoming, grads_out, grads_pre, grads_in = state_tuple
        micro_id = tick_id - (section_count - 1 - section_id)
        active = jnp.logical_and(micro_id >= 0, micro_id < MICRO)
        which_micro = jnp.clip(micro_id, 0, MICRO - 1)

        def run_block(stores):
            upstream = jnp.where(is_last, take_micro(last_micro, which_micro), incoming)
            in_grad, pre_grad = block_backward(
                upstream,
                take_micro(inputs_micro, which_micro),
                take_micro(preact_micro, which_micro),
                first_weight,
                second_weight,
            )
            updated = (
                store_micro(stores[0], upstream, which_micro),
                store_micro(stores[1], pre_grad, which_micro),
                store_micro(stores[2], in_grad, which_micro),
            )
            return (updated, in_grad)

        def skip_block(stores):
            return (stores, jnp.zeros_like(incoming))

        stores, passed = lax.cond(active, run_block, skip_block, (grads_out, grads_pre, grads_in))
        received = shifted(passed, "section", -1)
        return (received, stores[0], stores[1], stores[2])

    initial = (
        jnp.zeros((per_micro, width), jnp.bfloat16),
        jnp.zeros((MICRO, per_micro, width), jnp.bfloat16),
        jnp.zeros((MICRO, per_micro, preact.shape[1]), jnp.bfloat16),
        jnp.zeros((MICRO, per_micro, width), jnp.bfloat16),
    )
    final_state = lax.fori_loop(0, MICRO + section_count - 1, tick, initial)
    out_grads = final_state[1].reshape(row_count, width)
    pre_grads = final_state[2].reshape(row_count, preact.shape[1])
    in_grads = final_state[3].reshape(row_count, width)
    replica_count = lax.axis_size("replica")
    columns = normed
    first_sum = (
        lax.psum_scatter(
            lax.dot_general(
                columns, pre_grads, (((0,), (0,)), ((), ())), preferred_element_type=jnp.float32
            ).astype(jnp.bfloat16),
            "replica",
            scatter_dimension=0,
            tiled=True,
        ).astype(jnp.float32)
        / replica_count
    )
    columns = hidden
    second_sum = (
        lax.psum_scatter(
            lax.dot_general(
                columns, out_grads, (((0,), (0,)), ((), ())), preferred_element_type=jnp.float32
            ).astype(jnp.bfloat16),
            "replica",
            scatter_dimension=0,
            tiled=True,
        ).astype(jnp.float32)
        / replica_count
    )
    return (in_grads[None], first_sum[None], second_sum[None])


def solution(mesh):
    return jax.shard_map(
        local,
        mesh=mesh,
        in_specs=(
            P("section", "replica", None),
            P("section", "replica", None),
            P("section", "replica", None),
            P(),
            P("replica", None),
            P("replica", None),
            P(),
        ),
        out_specs=(
            P("section", "replica", None),
            P("section", "replica", None),
            P("section", "replica", None),
        ),
        check_vma=False,
    )
```

profile of v0, /device:TPU:2, one launch (start us, length us, event | category | flops | bytes accessed | tf_op | source)
XLA Modules:
  0.0 673.9 jit_solution(2133329231740861524)
XLA Ops:
  12.2 43.4 %all_gather.15 = bf16[256,512]{1,0:T(8,128)(2,1)S(1)} all-gather(bf16[8,512]{1,0:T(8,128)(2,1)S(1)} %convert_element_type.91), channel_id=1, replica_groups=mesh['section'=8,'replica'=32] {'replica'}, dimensions={0}, use_global_device_ids=true | all-gather | bytes 270336 | tf_op jit(solution)/shard_map/all_gather | solution.py:142
  57.3 26.2 %all-gather.5.cloned.1.call-done = bf16[1,1280,2560]{2,1,0:T(8,128)(2,1)} async-done(((bf16[1,40,2560]{2,1,0:T(8,128)(2,1)}), bf16[1,1280,2560]{2,1,0:T(8,128)(2,1)}) %all-gather.5.cloned.1.call-update) | async-done | bytes 6553616 | tf_op jit(solution)/shard_map/all_gather | solution.py:131
  83.6 7.4 %multiply_convert_fusion = (bf16[352,2560]{1,0:T(8,128)(2,1)}, f32[352,2560]{1,0:T(8,128)}) fusion(bf16[1,1280,2560]{2,1,0:T(8,128)(2,1)} %all-gather.5.cloned.1.call-done, bf16[1,352,1280]{2,1,0:T(8,128)(2,1)S(1)} %copy-done.2, f32[352]{0:T(512)S(1)} %add_rsqrt_fusion.2, f32[352]{0:T(512)S(1)} %broadcast_multiply_fusion.5), kind=kOutput, calls=%fused_computation.34 | convolution fusion | flops 2313175040 | bytes 12864256 | tf_op jit(solution)/shard_map/dot_general | solution.py:51
  90.9 63.3 %all-gather.7.cloned.1.call-done = bf16[1,2560,1280]{2,1,0:T(8,128)(2,1)} async-done(((bf16[1,80,1280]{2,1,0:T(8,128)(2,1)}), bf16[1,2560,1280]{2,1,0:T(8,128)(2,1)}) %all-gather.7.cloned.1.call-update) | async-done | bytes 6553616 | tf_op jit(solution)/shard_map/all_gather | solution.py:132
  154.2 6.0 fusion.71
  167.9 40.3 %all_gather.14 = bf16[256,512]{1,0:T(8,128)(2,1)S(1)} all-gather(bf16[8,512]{1,0:T(8,128)(2,1)S(1)} %multiply_convert_fusion.4), channel_id=1, replica_groups=mesh['section'=8,'replica'=32] {'replica'}, dimensions={0}, use_global_device_ids=true | all-gather | bytes 270336 | tf_op jit(solution)/shard_map/all_gather | solution.py:139
  211.7 2.8 reshape.133
  217.1 3.4 multiply_convert_fusion.1
  223.9 212.3 %while.21 = (s32[]{:T(128)}, bf16[88,1280]{1,0:T(8,128)(2,1)S(1)}, bf16[4,88,1280]{2,1,0:T(8,128)(2,1)}, bf16[4,88,2560]{2,1,0:T(8,128)(2,1)}, bf16[4,88,1280]{2...) while((s32[]{:T(128)}, bf16[88,1280]{1,0:T(8,128)(2,1)S(1)}, ...), condition=%wide.region_19.20_spmd, body=%wide.region_12.19_spmd.sunk | while | flops 1158277248 | bytes 46087640 | solution.py:203
  225.3 8.4 %collective-permute-done = bf16[88,1280]{1,0:T(8,128)(2,1)S(1)} collective-permute-done((bf16[88,1280]{1,0:T(8,128)(2,1)S(1)}, bf16[88,1280]{1,0:T(8,128)(2,1)S(1)}, u32[]{:S(2)}, u32[]{:S(2)}) %collective-permute-start) | collective-permute-done | bytes 225312 | tf_op jit(solution)/shard_map/while/body/eval_jaxpr/ppermute | solution.py:21
  235.0 7.6 %collective-permute-done = bf16[88,1280]{1,0:T(8,128)(2,1)S(1)} collective-permute-done((bf16[88,1280]{1,0:T(8,128)(2,1)S(1)}, bf16[88,1280]{1,0:T(8,128)(2,1)S(1)}, u32[]{:S(2)}, u32[]{:S(2)}) %collective-permute-start) | collective-permute-done | bytes 225312 | tf_op jit(solution)/shard_map/while/body/eval_jaxpr/ppermute | solution.py:21
  243.9 7.7 %collective-permute-done = bf16[88,1280]{1,0:T(8,128)(2,1)S(1)} collective-permute-done((bf16[88,1280]{1,0:T(8,128)(2,1)S(1)}, bf16[88,1280]{1,0:T(8,128)(2,1)S(1)}, u32[]{:S(2)}, u32[]{:S(2)}) %collective-permute-start) | collective-permute-done | bytes 225312 | tf_op jit(solution)/shard_map/while/body/eval_jaxpr/ppermute | solution.py:21
  252.9 7.2 %collective-permute-done = bf16[88,1280]{1,0:T(8,128)(2,1)S(1)} collective-permute-done((bf16[88,1280]{1,0:T(8,128)(2,1)S(1)}, bf16[88,1280]{1,0:T(8,128)(2,1)S(1)}, u32[]{:S(2)}, u32[]{:S(2)}) %collective-permute-start) | collective-permute-done | bytes 225312 | tf_op jit(solution)/shard_map/while/body/eval_jaxpr/ppermute | solution.py:21
  261.5 7.5 %collective-permute-done = bf16[88,1280]{1,0:T(8,128)(2,1)S(1)} collective-permute-done((bf16[88,1280]{1,0:T(8,128)(2,1)S(1)}, bf16[88,1280]{1,0:T(8,128)(2,1)S(1)}, u32[]{:S(2)}, u32[]{:S(2)}) %collective-permute-start) | collective-permute-done | bytes 225312 | tf_op jit(solution)/shard_map/while/body/eval_jaxpr/ppermute | solution.py:21
  270.3 7.5 %collective-permute-done = bf16[88,1280]{1,0:T(8,128)(2,1)S(1)} collective-permute-done((bf16[88,1280]{1,0:T(8,128)(2,1)S(1)}, bf16[88,1280]{1,0:T(8,128)(2,1)S(1)}, u32[]{:S(2)}, u32[]{:S(2)}) %collective-permute-start) | collective-permute-done | bytes 225312 | tf_op jit(solution)/shard_map/while/body/eval_jaxpr/ppermute | solution.py:21
  279.1 77.6 %collective-permute-done = bf16[88,1280]{1,0:T(8,128)(2,1)S(1)} collective-permute-done((bf16[88,1280]{1,0:T(8,128)(2,1)S(1)}, bf16[88,1280]{1,0:T(8,128)(2,1)S(1)}, u32[]{:S(2)}, u32[]{:S(2)}) %collective-permute-start) | collective-permute-done | bytes 225312 | tf_op jit(solution)/shard_map/while/body/eval_jaxpr/ppermute | solution.py:21
  356.7 11.3 %conditional.2 = (bf16[4,88,1280]{2,1,0:T(8,128)(2,1)}, bf16[4,88,2560]{2,1,0:T(8,128)(2,1)}, bf16[4,88,1280]{2,1,0:T(8,128)(2,1)}, bf16[88,1280]{1,0:T(8,128)(2,1)S(1)}) conditional(s32[]{:T(128)} %convert_element_type.179, (bf16[4,88,1280]{2,1,0:T(8,128)(2,1)}, bf16[4,88,2560]{2,1,0:T(8,128)(2,1)}, bf16[4,88,1280]{2,1,0:T(8,128)(2,1)}) %tuple.67, ...), branch_computations={%region_13.13_spmd, %region_14.18_spmd} | conditional | flops 1158277248 | bytes 45186188 | solution.py:193
  358.7 6.1 bitcast_dynamic-update-slice_fusion
  369.3 7.6 %collective-permute-done = bf16[88,1280]{1,0:T(8,128)(2,1)S(1)} collective-permute-done((bf16[88,1280]{1,0:T(8,128)(2,1)S(1)}, bf16[88,1280]{1,0:T(8,128)(2,1)S(1)}, u32[]{:S(2)}, u32[]{:S(2)}) %collective-permute-start) | collective-permute-done | bytes 225312 | tf_op jit(solution)/shard_map/while/body/eval_jaxpr/ppermute | solution.py:21
  376.8 11.3 %conditional.2 = (bf16[4,88,1280]{2,1,0:T(8,128)(2,1)}, bf16[4,88,2560]{2,1,0:T(8,128)(2,1)}, bf16[4,88,1280]{2,1,0:T(8,128)(2,1)}, bf16[88,1280]{1,0:T(8,128)(2,1)S(1)}) conditional(s32[]{:T(128)} %convert_element_type.179, (bf16[4,88,1280]{2,1,0:T(8,128)(2,1)}, bf16[4,88,2560]{2,1,0:T(8,128)(2,1)}, bf16[4,88,1280]{2,1,0:T(8,128)(2,1)}) %tuple.67, ...), branch_computations={%region_13.13_spmd, %region_14.18_spmd} | conditional | flops 1158277248 | bytes 45186188 | solution.py:193
  378.9 6.1 bitcast_dynamic-update-slice_fusion
  389.5 7.4 %collective-permute-done = bf16[88,1280]{1,0:T(8,128)(2,1)S(1)} collective-permute-done((bf16[88,1280]{1,0:T(8,128)(2,1)S(1)}, bf16[88,1280]{1,0:T(8,128)(2,1)S(1)}, u32[]{:S(2)}, u32[]{:S(2)}) %collective-permute-start) | collective-permute-done | bytes 225312 | tf_op jit(solution)/shard_map/while/body/eval_jaxpr/ppermute | solution.py:21
  396.9 11.3 %conditional.2 = (bf16[4,88,1280]{2,1,0:T(8,128)(2,1)}, bf16[4,88,2560]{2,1,0:T(8,128)(2,1)}, bf16[4,88,1280]{2,1,0:T(8,128)(2,1)}, bf16[88,1280]{1,0:T(8,128)(2,1)S(1)}) conditional(s32[]{:T(128)} %convert_element_type.179, (bf16[4,88,1280]{2,1,0:T(8,128)(2,1)}, bf16[4,88,2560]{2,1,0:T(8,128)(2,1)}, bf16[4,88,1280]{2,1,0:T(8,128)(2,1)}) %tuple.67, ...), branch_computations={%region_13.13_spmd, %region_14.18_spmd} | conditional | flops 1158277248 | bytes 45186188 | solution.py:193
  398.9 6.1 bitcast_dynamic-update-slice_fusion
  409.5 7.5 %collective-permute-done = bf16[88,1280]{1,0:T(8,128)(2,1)S(1)} collective-permute-done((bf16[88,1280]{1,0:T(8,128)(2,1)S(1)}, bf16[88,1280]{1,0:T(8,128)(2,1)S(1)}, u32[]{:S(2)}, u32[]{:S(2)}) %collective-permute-start) | collective-permute-done | bytes 225312 | tf_op jit(solution)/shard_map/while/body/eval_jaxpr/ppermute | solution.py:21
  417.0 11.3 %conditional.2 = (bf16[4,88,1280]{2,1,0:T(8,128)(2,1)}, bf16[4,88,2560]{2,1,0:T(8,128)(2,1)}, bf16[4,88,1280]{2,1,0:T(8,128)(2,1)}, bf16[88,1280]{1,0:T(8,128)(2,1)S(1)}) conditional(s32[]{:T(128)} %convert_element_type.179, (bf16[4,88,1280]{2,1,0:T(8,128)(2,1)}, bf16[4,88,2560]{2,1,0:T(8,128)(2,1)}, bf16[4,88,1280]{2,1,0:T(8,128)(2,1)}) %tuple.67, ...), branch_computations={%region_13.13_spmd, %region_14.18_spmd} | conditional | flops 1158277248 | bytes 45186188 | solution.py:193
  419.0 6.1 bitcast_dynamic-update-slice_fusion
  429.6 6.6 collective-permute-done
  436.2 8.1 %convolution_convert_fusion = bf16[2560,1280]{1,0:T(8,128)(2,1)} fusion(bf16[352,2560]{1,0:T(8,128)(2,1)} %get-tuple-element.406, bf16[352,1280]{1,0:T(8,128)(2,1)} %bitcast.106), kind=kOutput, calls=%fused_computation.32 | convolution fusion | flops 2310144000 | bytes 9256960 | tf_op jit(solution)/shard_map/dot_general | solution.py:223
  444.3 7.3 %convolution_convert_fusion.1 = bf16[1280,2560]{1,0:T(8,128)(2,1)} fusion(bf16[352,2560]{1,0:T(8,128)(2,1)} %bitcast.105, bf16[1,352,1280]{2,1,0:T(8,128)(2,1)S(1)} %bitcast.102, f32[352]{0:T(512)S(1)} %add_rsqrt_fusion.2, f32[352]{0:T(512)S(1)} %broadcast_multiply_fusion.5), kind=kOutput, calls=%fused_computation.33 | convolution fusion | flops 2311946240 | bytes 9259776 | tf_op jit(solution)/shard_map/dot_general | solution.py:211
  451.6 101.4 %reduce-scatter.5.cloned.1.call-done = bf16[80,1280]{1,0:T(8,128)(2,1)} async-done(((bf16[2560,1280]{1,0:T(8,128)(2,1)}), bf16[80,1280]{1,0:T(8,128)(2,1)}) %reduce-scatter.5.cloned.1.call-update) | async-done | bytes 204816 | tf_op jit(solution)/shard_map/reduce_scatter | solution.py:222
  554.7 111.0 %reduce-scatter.3.cloned.1.call-done = bf16[40,2560]{1,0:T(8,128)(2,1)} async-done(((bf16[1280,2560]{1,0:T(8,128)(2,1)}), bf16[40,2560]{1,0:T(8,128)(2,1)}) %reduce-scatter.3.cloned.1.call-update) | async-done | bytes 204816 | tf_op jit(solution)/shard_map/reduce_scatter | solution.py:210
  (118 shorter events, 62.7 us)
Async XLA Ops:
  7.2 160.3 %copy-start = (bf16[1280,512]{1,0:T(8,128)(2,1)S(1)}, bf16[1280,512]{1,0:T(8,128)(2,1)}, u32[]{:S(2)}) copy-start(bf16[1280,512]{1,0:T(8,128)(2,1)} %param.14) | copy-start | bytes 3932164
  7.2 49.8 %copy-start.2 = (bf16[1,352,1280]{2,1,0:T(8,128)(2,1)S(1)}, bf16[1,352,1280]{2,1,0:T(8,128)(2,1)}, u32[]{:S(2)}) copy-start(bf16[1,352,1280]{2,1,0:T(8,128)(2,1)} %param.11) | copy-start | bytes 2703364
  7.2 76.4 %all-gather.5.cloned.1.call-start = ((), (), s32[]{:S(2)}) async-start(), calls=%async_computation.4 | async-start | bytes 6758400 | tf_op jit(solution)/shard_map/all_gather | solution.py:131
  7.9 146.3 %all-gather.7.cloned.1.call-start = ((), (), s32[]{:S(2)}) async-start(), calls=%async_computation.5 | async-start | bytes 6758400 | tf_op jit(solution)/shard_map/all_gather | solution.py:132
  8.7 544.3 %reduce-scatter.5.cloned.1.call-start = ((), (), s32[]{:S(2)}) async-start(), calls=%async_computation.3 | async-start | bytes 6758400 | tf_op jit(solution)/shard_map/reduce_scatter | solution.py:222
  160.2 1.2 copy-start.3
  224.0 9.7 %collective-permute-start = (bf16[88,1280]{1,0:T(8,128)(2,1)S(1)}, bf16[88,1280]{1,0:T(8,128)(2,1)S(1)}, u32[]{:S(2)}, u32[]{:S(2)}) collective-permute-start(bf16[88,1280]{1,0:T(8,128)(2,1)S(1)} %get-tuple-element.494), channel_id=1, source_target_pairs={{32,0},{64,32},{96,64},{128,96},{160,128},{192,160},{224,192},{33,... | collective-permute-start | bytes 675848 | tf_op jit(solution)/shard_map/while/body/eval_jaxpr/ppermute | solution.py:21
  233.7 8.9 %collective-permute-start = (bf16[88,1280]{1,0:T(8,128)(2,1)S(1)}, bf16[88,1280]{1,0:T(8,128)(2,1)S(1)}, u32[]{:S(2)}, u32[]{:S(2)}) collective-permute-start(bf16[88,1280]{1,0:T(8,128)(2,1)S(1)} %get-tuple-element.494), channel_id=1, source_target_pairs={{32,0},{64,32},{96,64},{128,96},{160,128},{192,160},{224,192},{33,... | collective-permute-start | bytes 675848 | tf_op jit(solution)/shard_map/while/body/eval_jaxpr/ppermute | solution.py:21
  242.6 9.0 %collective-permute-start = (bf16[88,1280]{1,0:T(8,128)(2,1)S(1)}, bf16[88,1280]{1,0:T(8,128)(2,1)S(1)}, u32[]{:S(2)}, u32[]{:S(2)}) collective-permute-start(bf16[88,1280]{1,0:T(8,128)(2,1)S(1)} %get-tuple-element.494), channel_id=1, source_target_pairs={{32,0},{64,32},{96,64},{128,96},{160,128},{192,160},{224,192},{33,... | collective-permute-start | bytes 675848 | tf_op jit(solution)/shard_map/while/body/eval_jaxpr/ppermute | solution.py:21
  251.6 8.5 %collective-permute-start = (bf16[88,1280]{1,0:T(8,128)(2,1)S(1)}, bf16[88,1280]{1,0:T(8,128)(2,1)S(1)}, u32[]{:S(2)}, u32[]{:S(2)}) collective-permute-start(bf16[88,1280]{1,0:T(8,128)(2,1)S(1)} %get-tuple-element.494), channel_id=1, source_target_pairs={{32,0},{64,32},{96,64},{128,96},{160,128},{192,160},{224,192},{33,... | collective-permute-start | bytes 675848 | tf_op jit(solution)/shard_map/while/body/eval_jaxpr/ppermute | solution.py:21
  260.2 8.8 %collective-permute-start = (bf16[88,1280]{1,0:T(8,128)(2,1)S(1)}, bf16[88,1280]{1,0:T(8,128)(2,1)S(1)}, u32[]{:S(2)}, u32[]{:S(2)}) collective-permute-start(bf16[88,1280]{1,0:T(8,128)(2,1)S(1)} %get-tuple-element.494), channel_id=1, source_target_pairs={{32,0},{64,32},{96,64},{128,96},{160,128},{192,160},{224,192},{33,... | collective-permute-start | bytes 675848 | tf_op jit(solution)/shard_map/while/body/eval_jaxpr/ppermute | solution.py:21
  269.0 8.8 %collective-permute-start = (bf16[88,1280]{1,0:T(8,128)(2,1)S(1)}, bf16[88,1280]{1,0:T(8,128)(2,1)S(1)}, u32[]{:S(2)}, u32[]{:S(2)}) collective-permute-start(bf16[88,1280]{1,0:T(8,128)(2,1)S(1)} %get-tuple-element.494), channel_id=1, source_target_pairs={{32,0},{64,32},{96,64},{128,96},{160,128},{192,160},{224,192},{33,... | collective-permute-start | bytes 675848 | tf_op jit(solution)/shard_map/while/body/eval_jaxpr/ppermute | solution.py:21
  277.8 78.9 %collective-permute-start = (bf16[88,1280]{1,0:T(8,128)(2,1)S(1)}, bf16[88,1280]{1,0:T(8,128)(2,1)S(1)}, u32[]{:S(2)}, u32[]{:S(2)}) collective-permute-start(bf16[88,1280]{1,0:T(8,128)(2,1)S(1)} %get-tuple-element.494), channel_id=1, source_target_pairs={{32,0},{64,32},{96,64},{128,96},{160,128},{192,160},{224,192},{33,... | collective-permute-start | bytes 675848 | tf_op jit(solution)/shard_map/while/body/eval_jaxpr/ppermute | solution.py:21
  358.7 6.1 copy-start.1
  368.0 8.9 %collective-permute-start = (bf16[88,1280]{1,0:T(8,128)(2,1)S(1)}, bf16[88,1280]{1,0:T(8,128)(2,1)S(1)}, u32[]{:S(2)}, u32[]{:S(2)}) collective-permute-start(bf16[88,1280]{1,0:T(8,128)(2,1)S(1)} %get-tuple-element.494), channel_id=1, source_target_pairs={{32,0},{64,32},{96,64},{128,96},{160,128},{192,160},{224,192},{33,... | collective-permute-start | bytes 675848 | tf_op jit(solution)/shard_map/while/body/eval_jaxpr/ppermute | solution.py:21
  378.9 6.1 copy-start.1
  388.2 8.7 %collective-permute-start = (bf16[88,1280]{1,0:T(8,128)(2,1)S(1)}, bf16[88,1280]{1,0:T(8,128)(2,1)S(1)}, u32[]{:S(2)}, u32[]{:S(2)}) collective-permute-start(bf16[88,1280]{1,0:T(8,128)(2,1)S(1)} %get-tuple-element.494), channel_id=1, source_target_pairs={{32,0},{64,32},{96,64},{128,96},{160,128},{192,160},{224,192},{33,... | collective-permute-start | bytes 675848 | tf_op jit(solution)/shard_map/while/body/eval_jaxpr/ppermute | solution.py:21
  398.9 6.1 copy-start.1
  408.2 8.8 %collective-permute-start = (bf16[88,1280]{1,0:T(8,128)(2,1)S(1)}, bf16[88,1280]{1,0:T(8,128)(2,1)S(1)}, u32[]{:S(2)}, u32[]{:S(2)}) collective-permute-start(bf16[88,1280]{1,0:T(8,128)(2,1)S(1)} %get-tuple-element.494), channel_id=1, source_target_pairs={{32,0},{64,32},{96,64},{128,96},{160,128},{192,160},{224,192},{33,... | collective-permute-start | bytes 675848 | tf_op jit(solution)/shard_map/while/body/eval_jaxpr/ppermute | solution.py:21
  419.0 6.1 copy-start.1
  428.3 7.9 %collective-permute-start = (bf16[88,1280]{1,0:T(8,128)(2,1)S(1)}, bf16[88,1280]{1,0:T(8,128)(2,1)S(1)}, u32[]{:S(2)}, u32[]{:S(2)}) collective-permute-start(bf16[88,1280]{1,0:T(8,128)(2,1)S(1)} %get-tuple-element.494), channel_id=1, source_target_pairs={{32,0},{64,32},{96,64},{128,96},{160,128},{192,160},{224,192},{33,... | collective-permute-start | bytes 675848 | tf_op jit(solution)/shard_map/while/body/eval_jaxpr/ppermute | solution.py:21
  444.2 221.4 %reduce-scatter.3.cloned.1.call-start = ((), (), s32[]{:S(2)}) async-start(), calls=%async_computation.2 | async-start | bytes 6758400 | tf_op jit(solution)/shard_map/reduce_scatter | solution.py:210
Sparse Core Ops, SparseCore 0:
  10.6 72.9 all-gather.4
  86.1 68.0 all-gather.6
  444.4 108.5 reduce-scatter.4
  556.9 108.7 reduce-scatter.2
where the time goes:
time: 676 us; the launch traced here: 674 us
  waiting for transfers between devices  456 us (67%)
  blocking collectives  83.6 us (12%)
  matrix products  64.4 us (10%)
  other arithmetic  28.4 us (4%)
  starting transfers between devices  14.3 us (2%)
  between operations  13.9 us (2%)
  local copies, waits for them, and re-layouts  13.2 us (2%)
    ppermute x11, waiting for transfers between devices, shifted(): return lax.ppermute(block, axis, route)  152 us
    reduce_scatter x1, waiting for transfers between devices, local(): lax.psum_scatter(lax.dot_general(columns, pre_grads, (((0,), (0,)), ((),...  111 us
    reduce_scatter x1, waiting for transfers between devices, local(): lax.psum_scatter(lax.dot_general(columns, out_grads, (((0,), (0,)), ((),...  101 us
    all_gather x1, waiting for transfers between devices, local(): lax.all_gather(out_weight[0], 'replica', axis=0, tiled=True)  63.3 us
    all_gather x1, blocking collectives, local(): lax.all_gather(local_text.astype(jnp.bfloat16), 'replica', axis=0, tiled=...  43.4 us
    all_gather x1, blocking collectives, local(): lax.all_gather(audio_unit.astype(jnp.bfloat16), 'replica', axis=0, tiled=...  40.3 us
    all_gather x1, waiting for transfers between devices, local(): lax.all_gather(in_weight[0], 'replica', axis=0, tiled=True)  26.2 us
    dot_general x4, matrix products, block_backward(): lax.dot_general(out_grad, second_weight, (((1,), (1,)), ((), ())), prefer...  24.3 us
  transfers between devices with their start and end apart: 15, of which 15 were waited for; matrix products, arithmetic and copies ran while one was open for 3% of the time, Pallas kernels for 0%

commit v1 on v0

--- a/solution.py
+++ b/solution.py
@@ -6,6 +6,9 @@
 MICRO = 4
 FRAMES = 44
 
+HI = 4
+COL = 4
+CORE = 2
 
 eps_norm = 1e-05
 eps_unit = 1e-06
@@ -13,6 +16,133 @@
 grad_scale = 256.0
 sqrt_half = 0.7071067811865476
 inv_sqrt_two_pi = 0.3989422804014327
+
+
+def replica_of(hi, col, core):
+    return ((hi % HI) * COL + col % COL) * CORE + core % CORE
+
+
+def move(block, hi=0, col=0, core=0):
+    route = [
+        (replica_of(h, c, k), replica_of(h + hi, c + col, k + core))
+        for h in range(HI)
+        for c in range(COL)
+        for k in range(CORE)
+    ]
+    return lax.ppermute(block, "replica", route)
+
+
+def place():
+    replica = lax.axis_index("replica")
+    return replica // (COL * CORE), (replica // CORE) % COL, replica % CORE
+
+
+def in_order(own, from_back, axis_size, position):
+    ring = [from_back[2], from_back[1], from_back[0], own]
+    ring = jnp.stack(ring + ring[:3])
+    return lax.dynamic_slice_in_dim(ring, axis_size - 1 - position, axis_size, 0)
+
+
+def gather_hi(shard):
+    hi, _, _ = place()
+    return in_order(shard, [move(shard, hi=d) for d in (1, 2, 3)], HI, hi)
+
+
+def gather_weight(shard):
+    _, col, core = place()
+    stack = gather_hi(shard)
+    left = move(stack, col=1)
+    right = move(stack, col=-1)
+    far_low = move(left[:2], col=1)
+    far_high = move(right[2:], col=-1)
+    far = jnp.concatenate([far_low, far_high])
+    whole = jnp.zeros((HI, COL, CORE) + shard.shape, shard.dtype)
+    for blocks, where in (
+        (stack, col),
+        (left, (col + COL - 1) % COL),
+        (right, (col + 1) % COL),
+        (far, (col + 2) % COL),
+    ):
+        other = move(blocks, core=1)
+        for held, side in ((blocks, core), (other, 1 - core)):
+            whole = lax.dynamic_update_slice(
+                whole, held[:, None, None], (0, where, side, 0, 0)
+            )
+    return whole.reshape(HI * COL * CORE * shard.shape[0], shard.shape[1])
+
+
+def gather_small(shard):
+    hi, col, core = place()
+    other = move(shard, core=1)
+    pair = jnp.where(core == 0, jnp.stack([shard, other]), jnp.stack([other, shard]))
+    line = in_order(pair, [move(pair, col=d) for d in (1, 2, 3)], COL, col)
+    plane = in_order(line, [move(line, hi=d) for d in (1, 2, 3)], HI, hi)
+    return plane.reshape(-1, shard.shape[1])
+
+
+def half_columns(values):
+    _, col, _ = place()
+    rows, width = values.shape
+    part = width // (HI * COL * CORE)
+    turned = values.T.reshape(HI, COL, CORE, part, rows)
+    turned = turned.transpose(2, 1, 0, 3, 4)
+    return lax.dynamic_slice_in_dim(
+        jnp.concatenate([turned, turned[:, : COL - 1]], axis=1), col, COL, 1
+    )
+
+
+def chip_columns(values):
+    _, _, core = place()
+    halves = half_columns(values)
+    own = lax.dynamic_index_in_dim(halves, core, 0, keepdims=False)
+    given = lax.dynamic_index_in_dim(halves, 1 - core, 0, keepdims=False)
+    other = move(given, core=1)
+    return jnp.concatenate([own, other], axis=-1)
+
+
+def chip_rows(values):
+    return jnp.concatenate([values, move(values, core=1)], axis=0)
+
+
+def scatter_sum(left, right):
+    hi, _, _ = place()
+    part, rows = left.shape[2:]
+    width = right.shape[1]
+
+    def term(distance, halves=slice(None)):
+        chosen = left[distance, halves]
+        product = jnp.dot(
+            chosen.reshape(-1, rows), right, preferred_element_type=jnp.float32
+        )
+        return product.reshape(-1, part, width)
+
+    low, high = slice(0, 2), slice(2, 4)
+    far = term(2).astype(jnp.bfloat16)
+    far_low = move(far[:2], col=1)
+    far_high = move(far[2:], col=-1)
+    next_term = term(1)
+    back_term = term(3)
+    next_high = move(next_term[2:].astype(jnp.bfloat16), col=1)
+    back_low = move(back_term[:2].astype(jnp.bfloat16), col=-1)
+    next_low = move(
+        (next_term[:2] + far_low.astype(jnp.float32)).astype(jnp.bfloat16), col=1
+    )
+    back_high = move(
+        (back_term[2:] + far_high.astype(jnp.float32)).astype(jnp.bfloat16), col=-1
+    )
+    own = term(0)
+    total = jnp.concatenate(
+        [
+            own[:2] + next_low.astype(jnp.float32) + back_low.astype(jnp.float32),
+            own[2:] + next_high.astype(jnp.float32) + back_high.astype(jnp.float32),
+        ]
+    )
+    result = lax.dynamic_index_in_dim(total, hi, 0, keepdims=False)
+    rounded = total.astype(jnp.bfloat16)
+    for distance in (1, 2, 3):
+        given = lax.dynamic_index_in_dim(rounded, (hi + distance) % HI, 0, keepdims=False)
+        result = result + move(given, hi=distance).astype(jnp.float32)
+    return result / (HI * COL * CORE)
 
 
 def shifted(block, axis, distance):
@@ -127,22 +257,14 @@
     inputs = section_inputs[0]
     row_count = inputs.shape[0]
     per_micro = row_count // MICRO
-    first_weight, second_weight = (
-        lax.all_gather(in_weight[0], "replica", axis=0, tiled=True),
-        lax.all_gather(out_weight[0], "replica", axis=0, tiled=True),
-    )
+    first_weight = gather_weight(in_weight[0])
+    second_weight = gather_weight(out_weight[0])
+    local_text = paired_texts(text_embed, pair_label)
+    text_all = gather_small(local_text.astype(jnp.bfloat16)).astype(jnp.float32)
     normed, preact, hidden = block_front(inputs, first_weight)
     block_out = block_output(inputs, hidden, second_weight)
     audio_unit, inv_norm, centred, inv_std = audio_embed(block_out, projection, FRAMES)
-    local_text = paired_texts(text_embed, pair_label)
-    audio_all, text_all = (
-        lax.all_gather(audio_unit.astype(jnp.bfloat16), "replica", axis=0, tiled=True).astype(
-            audio_unit.dtype
-        ),
-        lax.all_gather(local_text.astype(jnp.bfloat16), "replica", axis=0, tiled=True).astype(
-            local_text.dtype
-        ),
-    )
+    audio_all = gather_small(audio_unit.astype(jnp.bfloat16)).astype(jnp.float32)
     clip_count = audio_unit.shape[0]
     first_clip = lax.axis_index("replica") * clip_count
     groups = jnp.repeat(pool_group, clip_count)
@@ -157,6 +279,8 @@
     last_grad = embed_backward(
         audio_grad, audio_unit, inv_norm, projection, centred, inv_std, FRAMES
     )
+    normed_columns = chip_columns(normed)
+    hidden_columns = chip_columns(hidden)
     section_count = lax.axis_size("section")
     section_id = lax.axis_index("section")
     is_last = section_id == section_count - 1
@@ -204,31 +328,8 @@
     out_grads = final_state[1].reshape(row_count, width)
     pre_grads = final_state[2].reshape(row_count, preact.shape[1])
     in_grads = final_state[3].reshape(row_count, width)
-    replica_count = lax.axis_size("replica")
-    columns = normed
-    first_sum = (
-        lax.psum_scatter(
-            lax.dot_general(
-                columns, pre_grads, (((0,), (0,)), ((), ())), preferred_element_type=jnp.float32
-            ).astype(jnp.bfloat16),
-            "replica",
-            scatter_dimension=0,
-            tiled=True,
-        ).astype(jnp.float32)
-        / replica_count
-    )
-    columns = hidden
-    second_sum = (
-        lax.psum_scatter(
-            lax.dot_general(
-                columns, out_grads, (((0,), (0,)), ((), ())), preferred_element_type=jnp.float32
-            ).astype(jnp.bfloat16),
-            "replica",
-            scatter_dimension=0,
-            tiled=True,
-        ).astype(jnp.float32)
-        / replica_count
-    )
+    second_sum = scatter_sum(hidden_columns, chip_rows(out_grads))
+    first_sum = scatter_sum(normed_columns, chip_rows(pre_grads))
     return (in_grads[None], first_sum[None], second_sum[None])
 
 

time: 676 us -> 509 us (0.75); the launches traced: 674 us -> 500 us
  waiting for transfers between devices: 456 us -> 263 us
  starting transfers between devices: 14.3 us -> 118 us
  blocking collectives: 83.6 us -> 0 us
  local copies, waits for them, and re-layouts: 13.2 us -> 26.4 us
  between operations: 13.9 us -> 2.34 us
  matrix products: 64.4 us -> 56 us
    reduce_scatter x2 -> x0, waiting for transfers between devices: 212 us -> none  [the longest x1 111 us: local(): lax.psum_scatter(lax.dot_general(columns, pre_grads, (((0,), (0,)), ((),...]
    ppermute x0 -> x58, waiting for transfers between devices: none -> 116 us  [move(): return lax.ppermute(block, 'replica', route)]
    ppermute x0 -> x58, starting transfers between devices: none -> 104 us  [move(): return lax.ppermute(block, 'replica', route)]
    all_gather x2 -> x0, waiting for transfers between devices: 89.5 us -> none  [the longest x1 63.3 us: local(): lax.all_gather(out_weight[0], 'replica', axis=0, tiled=True)]
    all_gather x2 -> x0, blocking collectives: 83.6 us -> none  [the longest x1 43.4 us: local(): lax.all_gather(local_text.astype(jnp.bfloat16), 'replica', axis=0, tiled=...]
    dot_general x2 -> x8, matrix products: 15.3 us -> 13.5 us  [term(): jnp.dot(chosen.reshape(-1, rows), right, preferred_element_type=jnp.float32)]
  transfers between devices with their start and end apart: 15 -> 69, of which waited for: 15 -> 40; matrix products, arithmetic and copies ran while one was open for 3% -> 20% of each run, Pallas kernels for 0% -> 0%
where the time goes in v1:
time: 509 us; the launch traced here: 500 us
  waiting for transfers between devices  263 us (52%)
  starting transfers between devices  118 us (23%)
  matrix products  56 us (11%)
  other arithmetic  33.6 us (7%)
  local copies, waits for them, and re-layouts  26.4 us (5%)
    ppermute x11, waiting for transfers between devices, shifted(): return lax.ppermute(block, axis, route)  147 us
    ppermute x58, waiting for transfers between devices, move(): return lax.ppermute(block, 'replica', route)  116 us
    ppermute x58, starting transfers between devices, move(): return lax.ppermute(block, 'replica', route)  104 us
    dot_general x4, matrix products, block_backward(): lax.dot_general(out_grad, second_weight, (((1,), (1,)), ((), ())), prefer...  24.3 us
    ppermute x11, starting transfers between devices, shifted(): return lax.ppermute(block, axis, route)  14.2 us
    dot_general x8, matrix products, term(): jnp.dot(chosen.reshape(-1, rows), right, preferred_element_type=jnp.float32)  13.5 us
    dynamic_update_slice x8, other arithmetic, store_micro(): return lax.dynamic_update_index_in_dim(stacked, update, which_micro, 0)  10.6 us
  transfers between devices with their start and end apart: 69, of which 40 were waited for; matrix products, arithmetic and copies ran while one was open for 20% of the time, Pallas kernels for 0%

profile of v1, /device:TPU:2, one launch (start us, length us, event | category | flops | bytes accessed | tf_op | source)
XLA Modules:
  0.0 499.5 jit_solution(13616336030128792677)
XLA Ops:
  0.7 6.4 %collective-permute-start.12 = (bf16[80,1280]{1,0:T(8,128)(2,1)}, bf16[80,1280]{1,0:T(8,128)(2,1)S(1)}, u32[]{:S(2)}, u32[]{:S(2)}) collective-permute-start(bf16[80,1280]{1,0:T(8,128)(2,1)} %bitcast.357), channel_id=1, source_target_pairs={{0,24},{1,25},{2,26},{3,27},{4,28},{5,29},{6,30},{7,31},{8,0},{9,1... | collective-permute-start | bytes 614408 | tf_op jit(solution)/shard_map/ppermute | solution.py:32
  30.6 6.0 %collective-permute-start.36 = (bf16[4,2,8,512]{3,2,1,0:T(8,128)(2,1)S(1)}, bf16[4,2,8,512]{3,2,1,0:T(8,128)(2,1)S(1)}, u32[]{:S(2)}, u32[]{:S(2)}) collective-permute-start(bf16[4,2,8,512]{3,2,1,0:T(8,128)(2,1)S(1)} %constant_dynamic-slice_fusion.2), channel_id=1, source_target_pairs={{0,8},{1,9},{2,10},{3,11},{4,12},{5,13},{6,14},{7,15},{8,16},{9,17... | collective-permute-start | bytes 196616 | tf_op jit(solution)/shard_map/ppermute | solution.py:32
  45.8 9.7 %collective-permute-start.18 = (bf16[4,80,1280]{2,1,0:T(8,128)(2,1)S(1)}, bf16[4,80,1280]{2,1,0:T(8,128)(2,1)S(1)}, u32[]{:S(2)}, u32[]{:S(2)}) collective-permute-start(bf16[4,80,1280]{2,1,0:T(8,128)(2,1)S(1)} %get-tuple-element.402), channel_id=1, source_target_pairs={{0,6},{1,7},{2,0},{3,1},{4,2},{5,3},{6,4},{7,5},{8,14},{9,15},{10,... | collective-permute-start | bytes 2457608 | tf_op jit(solution)/shard_map/ppermute | solution.py:32
  60.0 6.1 %collective-permute-done.16 = bf16[4,80,1280]{2,1,0:T(8,128)(2,1)S(1)} collective-permute-done((bf16[4,80,1280]{2,1,0:T(8,128)(2,1)S(1)}, bf16[4,80,1280]{2,1,0:T(8,128)(2,1)S(1)}, u32[]{:S(2)}, u32[]{:S(2)}) %collective-permute-start.16) | collective-permute-done | bytes 819232 | tf_op jit(solution)/shard_map/ppermute | solution.py:32
  66.2 8.0 %collective-permute-done.18 = bf16[4,80,1280]{2,1,0:T(8,128)(2,1)S(1)} collective-permute-done((bf16[4,80,1280]{2,1,0:T(8,128)(2,1)S(1)}, bf16[4,80,1280]{2,1,0:T(8,128)(2,1)S(1)}, u32[]{:S(2)}, u32[]{:S(2)}) %collective-permute-start.18) | collective-permute-done | bytes 819232 | tf_op jit(solution)/shard_map/ppermute | solution.py:32
  77.4 6.3 %collective-permute-done.5 = bf16[4,40,2560]{2,1,0:T(8,128)(2,1)S(1)} collective-permute-done((bf16[4,40,2560]{2,1,0:T(8,128)(2,1)S(1)}, bf16[4,40,2560]{2,1,0:T(8,128)(2,1)S(1)}, u32[]{:S(2)}, u32[]{:S(2)}) %collective-permute-start.5) | collective-permute-done | bytes 819232 | tf_op jit(solution)/shard_map/ppermute | solution.py:32
  137.5 5.8 %collective-permute-start.27 = (bf16[4,2,8,512]{3,2,1,0:T(8,128)(2,1)S(1)}, bf16[4,2,8,512]{3,2,1,0:T(8,128)(2,1)S(1)}, u32[]{:S(2)}, u32[]{:S(2)}) collective-permute-start(bf16[4,2,8,512]{3,2,1,0:T(8,128)(2,1)S(1)} %constant_dynamic-slice_fusion.4), channel_id=1, source_target_pairs={{0,24},{1,25},{2,26},{3,27},{4,28},{5,29},{6,30},{7,31},{8,0},{9,1... | collective-permute-start | bytes 196616 | tf_op jit(solution)/shard_map/ppermute | solution.py:32
  171.9 206.4 %while.21 = (s32[]{:T(128)}, bf16[88,1280]{1,0:T(8,128)(2,1)S(1)}, bf16[4,88,1280]{2,1,0:T(8,128)(2,1)}, bf16[4,88,2560]{2,1,0:T(8,128)(2,1)}, bf16[4,88,1280]{2...) while((s32[]{:T(128)}, bf16[88,1280]{1,0:T(8,128)(2,1)S(1)}, ...), condition=%wide.region_19.20_spmd, body=%wide.region_12.19_spmd.sunk | while | flops 1158277248 | bytes 46087640 | solution.py:327
  173.3 7.8 %collective-permute-done = bf16[88,1280]{1,0:T(8,128)(2,1)S(1)} collective-permute-done((bf16[88,1280]{1,0:T(8,128)(2,1)S(1)}, bf16[88,1280]{1,0:T(8,128)(2,1)S(1)}, u32[]{:S(2)}, u32[]{:S(2)}) %collective-permute-start) | collective-permute-done | bytes 225312 | tf_op jit(solution)/shard_map/while/body/eval_jaxpr/ppermute | solution.py:151
  182.4 6.9 %collective-permute-done = bf16[88,1280]{1,0:T(8,128)(2,1)S(1)} collective-permute-done((bf16[88,1280]{1,0:T(8,128)(2,1)S(1)}, bf16[88,1280]{1,0:T(8,128)(2,1)S(1)}, u32[]{:S(2)}, u32[]{:S(2)}) %collective-permute-start) | collective-permute-done | bytes 225312 | tf_op jit(solution)/shard_map/while/body/eval_jaxpr/ppermute | solution.py:151
  190.6 7.1 %collective-permute-done = bf16[88,1280]{1,0:T(8,128)(2,1)S(1)} collective-permute-done((bf16[88,1280]{1,0:T(8,128)(2,1)S(1)}, bf16[88,1280]{1,0:T(8,128)(2,1)S(1)}, u32[]{:S(2)}, u32[]{:S(2)}) %collective-permute-start) | collective-permute-done | bytes 225312 | tf_op jit(solution)/shard_map/while/body/eval_jaxpr/ppermute | solution.py:151
  199.0 7.5 %collective-permute-done = bf16[88,1280]{1,0:T(8,128)(2,1)S(1)} collective-permute-done((bf16[88,1280]{1,0:T(8,128)(2,1)S(1)}, bf16[88,1280]{1,0:T(8,128)(2,1)S(1)}, u32[]{:S(2)}, u32[]{:S(2)}) %collective-permute-start) | collective-permute-done | bytes 225312 | tf_op jit(solution)/shard_map/while/body/eval_jaxpr/ppermute | solution.py:151
  207.9 7.5 %collective-permute-done = bf16[88,1280]{1,0:T(8,128)(2,1)S(1)} collective-permute-done((bf16[88,1280]{1,0:T(8,128)(2,1)S(1)}, bf16[88,1280]{1,0:T(8,128)(2,1)S(1)}, u32[]{:S(2)}, u32[]{:S(2)}) %collective-permute-start) | collective-permute-done | bytes 225312 | tf_op jit(solution)/shard_map/while/body/eval_jaxpr/ppermute | solution.py:151
  216.7 7.5 %collective-permute-done = bf16[88,1280]{1,0:T(8,128)(2,1)S(1)} collective-permute-done((bf16[88,1280]{1,0:T(8,128)(2,1)S(1)}, bf16[88,1280]{1,0:T(8,128)(2,1)S(1)}, u32[]{:S(2)}, u32[]{:S(2)}) %collective-permute-start) | collective-permute-done | bytes 225312 | tf_op jit(solution)/shard_map/while/body/eval_jaxpr/ppermute | solution.py:151
  225.5 73.4 %collective-permute-done = bf16[88,1280]{1,0:T(8,128)(2,1)S(1)} collective-permute-done((bf16[88,1280]{1,0:T(8,128)(2,1)S(1)}, bf16[88,1280]{1,0:T(8,128)(2,1)S(1)}, u32[]{:S(2)}, u32[]{:S(2)}) %collective-permute-start) | collective-permute-done | bytes 225312 | tf_op jit(solution)/shard_map/while/body/eval_jaxpr/ppermute | solution.py:151
  298.9 11.3 %conditional.2 = (bf16[4,88,1280]{2,1,0:T(8,128)(2,1)}, bf16[4,88,2560]{2,1,0:T(8,128)(2,1)}, bf16[4,88,1280]{2,1,0:T(8,128)(2,1)}, bf16[88,1280]{1,0:T(8,128)(2,1)S(1)}) conditional(s32[]{:T(128)} %convert_element_type.336, (bf16[4,88,1280]{2,1,0:T(8,128)(2,1)}, bf16[4,88,2560]{2,1,0:T(8,128)(2,1)}, bf16[4,88,1280]{2,1,0:T(8,128)(2,1)}) %tuple.83, ...), branch_computations={%region_13.13_spmd, %region_14.18_spmd} | conditional | flops 1158277248 | bytes 45186188 | solution.py:317
  300.9 6.1 %bitcast_dynamic-update-slice_fusion = (bf16[4,88,2560]{2,1,0:T(8,128)(2,1)}, bf16[88,2560]{1,0:T(8,128)(2,1)S(1)}) fusion(bf16[4,88,2560]{2,1,0:T(8,128)(2,1)} %get-tuple-element.337, s32[]{:T(128)S(6)} %min.10, f32[4,88,2560]{2,1,0:T(8,128)} %get-tuple-element.339, bf16[88,1280]{1,0:T(8,128)(2,1)S(1)} %get-tuple-element.400, ...), kind=kOutput, calls=%fused_computation.24 | convolution fusion | flops 578969600 | bytes 8581124 | tf_op jit(solution)/shard_map/while/body/eval_jaxpr/cond/branch_1_fun/dot_general | solution.py:193
  311.5 7.5 %collective-permute-done = bf16[88,1280]{1,0:T(8,128)(2,1)S(1)} collective-permute-done((bf16[88,1280]{1,0:T(8,128)(2,1)S(1)}, bf16[88,1280]{1,0:T(8,128)(2,1)S(1)}, u32[]{:S(2)}, u32[]{:S(2)}) %collective-permute-start) | collective-permute-done | bytes 225312 | tf_op jit(solution)/shard_map/while/body/eval_jaxpr/ppermute | solution.py:151
  319.0 11.3 %conditional.2 = (bf16[4,88,1280]{2,1,0:T(8,128)(2,1)}, bf16[4,88,2560]{2,1,0:T(8,128)(2,1)}, bf16[4,88,1280]{2,1,0:T(8,128)(2,1)}, bf16[88,1280]{1,0:T(8,128)(2,1)S(1)}) conditional(s32[]{:T(128)} %convert_element_type.336, (bf16[4,88,1280]{2,1,0:T(8,128)(2,1)}, bf16[4,88,2560]{2,1,0:T(8,128)(2,1)}, bf16[4,88,1280]{2,1,0:T(8,128)(2,1)}) %tuple.83, ...), branch_computations={%region_13.13_spmd, %region_14.18_spmd} | conditional | flops 1158277248 | bytes 45186188 | solution.py:317
  321.1 6.1 %bitcast_dynamic-update-slice_fusion = (bf16[4,88,2560]{2,1,0:T(8,128)(2,1)}, bf16[88,2560]{1,0:T(8,128)(2,1)S(1)}) fusion(bf16[4,88,2560]{2,1,0:T(8,128)(2,1)} %get-tuple-element.337, s32[]{:T(128)S(6)} %min.10, f32[4,88,2560]{2,1,0:T(8,128)} %get-tuple-element.339, bf16[88,1280]{1,0:T(8,128)(2,1)S(1)} %get-tuple-element.400, ...), kind=kOutput, calls=%fused_computation.24 | convolution fusion | flops 578969600 | bytes 8581124 | tf_op jit(solution)/shard_map/while/body/eval_jaxpr/cond/branch_1_fun/dot_general | solution.py:193
  331.6 7.5 %collective-permute-done = bf16[88,1280]{1,0:T(8,128)(2,1)S(1)} collective-permute-done((bf16[88,1280]{1,0:T(8,128)(2,1)S(1)}, bf16[88,1280]{1,0:T(8,128)(2,1)S(1)}, u32[]{:S(2)}, u32[]{:S(2)}) %collective-permute-start) | collective-permute-done | bytes 225312 | tf_op jit(solution)/shard_map/while/body/eval_jaxpr/ppermute | solution.py:151
  339.1 11.3 %conditional.2 = (bf16[4,88,1280]{2,1,0:T(8,128)(2,1)}, bf16[4,88,2560]{2,1,0:T(8,128)(2,1)}, bf16[4,88,1280]{2,1,0:T(8,128)(2,1)}, bf16[88,1280]{1,0:T(8,128)(2,1)S(1)}) conditional(s32[]{:T(128)} %convert_element_type.336, (bf16[4,88,1280]{2,1,0:T(8,128)(2,1)}, bf16[4,88,2560]{2,1,0:T(8,128)(2,1)}, bf16[4,88,1280]{2,1,0:T(8,128)(2,1)}) %tuple.83, ...), branch_computations={%region_13.13_spmd, %region_14.18_spmd} | conditional | flops 1158277248 | bytes 45186188 | solution.py:317
  341.1 6.1 %bitcast_dynamic-update-slice_fusion = (bf16[4,88,2560]{2,1,0:T(8,128)(2,1)}, bf16[88,2560]{1,0:T(8,128)(2,1)S(1)}) fusion(bf16[4,88,2560]{2,1,0:T(8,128)(2,1)} %get-tuple-element.337, s32[]{:T(128)S(6)} %min.10, f32[4,88,2560]{2,1,0:T(8,128)} %get-tuple-element.339, bf16[88,1280]{1,0:T(8,128)(2,1)S(1)} %get-tuple-element.400, ...), kind=kOutput, calls=%fused_computation.24 | convolution fusion | flops 578969600 | bytes 8581124 | tf_op jit(solution)/shard_map/while/body/eval_jaxpr/cond/branch_1_fun/dot_general | solution.py:193
  351.7 7.5 %collective-permute-done = bf16[88,1280]{1,0:T(8,128)(2,1)S(1)} collective-permute-done((bf16[88,1280]{1,0:T(8,128)(2,1)S(1)}, bf16[88,1280]{1,0:T(8,128)(2,1)S(1)}, u32[]{:S(2)}, u32[]{:S(2)}) %collective-permute-start) | collective-permute-done | bytes 225312 | tf_op jit(solution)/shard_map/while/body/eval_jaxpr/ppermute | solution.py:151
  359.1 11.3 %conditional.2 = (bf16[4,88,1280]{2,1,0:T(8,128)(2,1)}, bf16[4,88,2560]{2,1,0:T(8,128)(2,1)}, bf16[4,88,1280]{2,1,0:T(8,128)(2,1)}, bf16[88,1280]{1,0:T(8,128)(2,1)S(1)}) conditional(s32[]{:T(128)} %convert_element_type.336, (bf16[4,88,1280]{2,1,0:T(8,128)(2,1)}, bf16[4,88,2560]{2,1,0:T(8,128)(2,1)}, bf16[4,88,1280]{2,1,0:T(8,128)(2,1)}) %tuple.83, ...), branch_computations={%region_13.13_spmd, %region_14.18_spmd} | conditional | flops 1158277248 | bytes 45186188 | solution.py:317
  361.2 6.1 %bitcast_dynamic-update-slice_fusion = (bf16[4,88,2560]{2,1,0:T(8,128)(2,1)}, bf16[88,2560]{1,0:T(8,128)(2,1)S(1)}) fusion(bf16[4,88,2560]{2,1,0:T(8,128)(2,1)} %get-tuple-element.337, s32[]{:T(128)S(6)} %min.10, f32[4,88,2560]{2,1,0:T(8,128)} %get-tuple-element.339, bf16[88,1280]{1,0:T(8,128)(2,1)S(1)} %get-tuple-element.400, ...), kind=kOutput, calls=%fused_computation.24 | convolution fusion | flops 578969600 | bytes 8581124 | tf_op jit(solution)/shard_map/while/body/eval_jaxpr/cond/branch_1_fun/dot_general | solution.py:193
  371.7 6.6 %collective-permute-done = bf16[88,1280]{1,0:T(8,128)(2,1)S(1)} collective-permute-done((bf16[88,1280]{1,0:T(8,128)(2,1)S(1)}, bf16[88,1280]{1,0:T(8,128)(2,1)S(1)}, u32[]{:S(2)}, u32[]{:S(2)}) %collective-permute-start) | collective-permute-done | bytes 225312 | tf_op jit(solution)/shard_map/while/body/eval_jaxpr/ppermute | solution.py:151
  402.6 5.5 %collective-permute-done.54 = bf16[2,80,1280]{2,1,0:T(8,128)(2,1)S(1)} collective-permute-done((bf16[2,80,1280]{2,1,0:T(8,128)(2,1)S(1)}, bf16[2,80,1280]{2,1,0:T(8,128)(2,1)S(1)}, u32[]{:S(2)}, u32[]{:S(2)}) %collective-permute-start.54) | collective-permute-done | bytes 409632 | tf_op jit(solution)/shard_map/ppermute | solution.py:32
  410.3 7.7 %collective-permute-done.50 = bf16[2,80,1280]{2,1,0:T(8,128)(2,1)S(1)} collective-permute-done((bf16[2,80,1280]{2,1,0:T(8,128)(2,1)S(1)}, bf16[2,80,1280]{2,1,0:T(8,128)(2,1)S(1)}, u32[]{:S(2)}, u32[]{:S(2)}) %collective-permute-start.50) | collective-permute-done | bytes 409632 | tf_op jit(solution)/shard_map/ppermute | solution.py:32
  418.5 6.6 %collective-permute-done.55 = bf16[2,80,1280]{2,1,0:T(8,128)(2,1)S(1)} collective-permute-done((bf16[2,80,1280]{2,1,0:T(8,128)(2,1)S(1)}, bf16[2,80,1280]{2,1,0:T(8,128)(2,1)S(1)}, u32[]{:S(2)}, u32[]{:S(2)}) %collective-permute-start.55) | collective-permute-done | bytes 409632 | tf_op jit(solution)/shard_map/ppermute | solution.py:32
  448.8 10.9 %collective-permute-done.39 = bf16[2,40,2560]{2,1,0:T(8,128)(2,1)S(1)} collective-permute-done((bf16[2,40,2560]{2,1,0:T(8,128)(2,1)S(1)}, bf16[2,40,2560]{2,1,0:T(8,128)(2,1)S(1)}, u32[]{:S(2)}, u32[]{:S(2)}) %collective-permute-start.39) | collective-permute-done | bytes 409632 | tf_op jit(solution)/shard_map/ppermute | solution.py:32
  461.7 10.6 %collective-permute-done.44 = bf16[2,40,2560]{2,1,0:T(8,128)(2,1)S(1)} collective-permute-done((bf16[2,40,2560]{2,1,0:T(8,128)(2,1)S(1)}, bf16[2,40,2560]{2,1,0:T(8,128)(2,1)S(1)}, u32[]{:S(2)}, u32[]{:S(2)}) %collective-permute-start.44) | collective-permute-done | bytes 409632 | tf_op jit(solution)/shard_map/ppermute | solution.py:32
  (373 shorter events, 236.7 us)
Async XLA Ops:
  0.7 41.7 %collective-permute-start.12 = (bf16[80,1280]{1,0:T(8,128)(2,1)}, bf16[80,1280]{1,0:T(8,128)(2,1)S(1)}, u32[]{:S(2)}, u32[]{:S(2)}) collective-permute-start(bf16[80,1280]{1,0:T(8,128)(2,1)} %bitcast.357), channel_id=1, source_target_pairs={{0,24},{1,25},{2,26},{3,27},{4,28},{5,29},{6,30},{7,31},{8,0},{9,1... | collective-permute-start | bytes 614408 | tf_op jit(solution)/shard_map/ppermute | solution.py:32
  7.0 36.0 %collective-permute-start.13 = (bf16[80,1280]{1,0:T(8,128)(2,1)}, bf16[80,1280]{1,0:T(8,128)(2,1)S(1)}, u32[]{:S(2)}, u32[]{:S(2)}) collective-permute-start(bf16[80,1280]{1,0:T(8,128)(2,1)} %bitcast.358), channel_id=1, source_target_pairs={{0,16},{1,17},{2,18},{3,19},{4,20},{5,21},{6,22},{7,23},{8,24},{9,... | collective-permute-start | bytes 614408 | tf_op jit(solution)/shard_map/ppermute | solution.py:32
  8.0 35.0 %collective-permute-start.14 = (bf16[80,1280]{1,0:T(8,128)(2,1)}, bf16[80,1280]{1,0:T(8,128)(2,1)S(1)}, u32[]{:S(2)}, u32[]{:S(2)}) collective-permute-start(bf16[80,1280]{1,0:T(8,128)(2,1)} %bitcast.359), channel_id=1, source_target_pairs={{0,8},{1,9},{2,10},{3,11},{4,12},{5,13},{6,14},{7,15},{8,16},{9,17... | collective-permute-start | bytes 614408 | tf_op jit(solution)/shard_map/ppermute | solution.py:32
  39.0 16.5 %collective-permute-start.2 = (bf16[40,2560]{1,0:T(8,128)(2,1)S(1)}, bf16[40,2560]{1,0:T(8,128)(2,1)S(1)}, u32[]{:S(2)}, u32[]{:S(2)}) collective-permute-start(bf16[40,2560]{1,0:T(8,128)(2,1)S(1)} %bitcast.361), channel_id=1, source_target_pairs={{0,16},{1,17},{2,18},{3,19},{4,20},{5,21},{6,22},{7,23},{8,24},{9,... | collective-permute-start | bytes 614408 | tf_op jit(solution)/shard_map/ppermute | solution.py:32
  42.4 13.1 %collective-permute-start.3 = (bf16[40,2560]{1,0:T(8,128)(2,1)S(1)}, bf16[40,2560]{1,0:T(8,128)(2,1)S(1)}, u32[]{:S(2)}, u32[]{:S(2)}) collective-permute-start(bf16[40,2560]{1,0:T(8,128)(2,1)S(1)} %bitcast.362), channel_id=1, source_target_pairs={{0,8},{1,9},{2,10},{3,11},{4,12},{5,13},{6,14},{7,15},{8,16},{9,17... | collective-permute-start | bytes 614408 | tf_op jit(solution)/shard_map/ppermute | solution.py:32
  44.0 43.1 %collective-permute-start.15 = (bf16[4,80,1280]{2,1,0:T(8,128)(2,1)S(1)}, bf16[4,80,1280]{2,1,0:T(8,128)(2,1)S(1)}, u32[]{:S(2)}, u32[]{:S(2)}) collective-permute-start(bf16[4,80,1280]{2,1,0:T(8,128)(2,1)S(1)} %get-tuple-element.402), channel_id=1, source_target_pairs={{0,1},{1,0},{2,3},{3,2},{4,5},{5,4},{6,7},{7,6},{8,9},{9,8},{10,11... | collective-permute-start | bytes 2457608 | tf_op jit(solution)/shard_map/ppermute | solution.py:32
  44.1 22.0 %collective-permute-start.16 = (bf16[4,80,1280]{2,1,0:T(8,128)(2,1)S(1)}, bf16[4,80,1280]{2,1,0:T(8,128)(2,1)S(1)}, u32[]{:S(2)}, u32[]{:S(2)}) collective-permute-start(bf16[4,80,1280]{2,1,0:T(8,128)(2,1)S(1)} %get-tuple-element.402), channel_id=1, source_target_pairs={{0,2},{1,3},{2,4},{3,5},{4,6},{5,7},{6,0},{7,1},{8,10},{9,11},{10,... | collective-permute-start | bytes 2457608 | tf_op jit(solution)/shard_map/ppermute | solution.py:32
  45.8 28.4 %collective-permute-start.18 = (bf16[4,80,1280]{2,1,0:T(8,128)(2,1)S(1)}, bf16[4,80,1280]{2,1,0:T(8,128)(2,1)S(1)}, u32[]{:S(2)}, u32[]{:S(2)}) collective-permute-start(bf16[4,80,1280]{2,1,0:T(8,128)(2,1)S(1)} %get-tuple-element.402), channel_id=1, source_target_pairs={{0,6},{1,7},{2,0},{3,1},{4,2},{5,3},{6,4},{7,5},{8,14},{9,15},{10,... | collective-permute-start | bytes 2457608 | tf_op jit(solution)/shard_map/ppermute | solution.py:32
  56.5 27.1 %collective-permute-start.5 = (bf16[4,40,2560]{2,1,0:T(8,128)(2,1)S(1)}, bf16[4,40,2560]{2,1,0:T(8,128)(2,1)S(1)}, u32[]{:S(2)}, u32[]{:S(2)}) collective-permute-start(bf16[4,40,2560]{2,1,0:T(8,128)(2,1)S(1)} %get-tuple-element.404), channel_id=1, source_target_pairs={{0,2},{1,3},{2,4},{3,5},{4,6},{5,7},{6,0},{7,1},{8,10},{9,11},{10,... | collective-permute-start | bytes 2457608 | tf_op jit(solution)/shard_map/ppermute | solution.py:32
  56.6 30.3 %collective-permute-start.7 = (bf16[4,40,2560]{2,1,0:T(8,128)(2,1)S(1)}, bf16[4,40,2560]{2,1,0:T(8,128)(2,1)S(1)}, u32[]{:S(2)}, u32[]{:S(2)}) collective-permute-start(bf16[4,40,2560]{2,1,0:T(8,128)(2,1)S(1)} %get-tuple-element.404), channel_id=1, source_target_pairs={{0,6},{1,7},{2,0},{3,1},{4,2},{5,3},{6,4},{7,5},{8,14},{9,15},{10,... | collective-permute-start | bytes 2457608 | tf_op jit(solution)/shard_map/ppermute | solution.py:32
  66.1 23.1 %collective-permute-start.4 = (bf16[4,40,2560]{2,1,0:T(8,128)(2,1)S(1)}, bf16[4,40,2560]{2,1,0:T(8,128)(2,1)S(1)}, u32[]{:S(2)}, u32[]{:S(2)}) collective-permute-start(bf16[4,40,2560]{2,1,0:T(8,128)(2,1)S(1)} %get-tuple-element.404), channel_id=1, source_target_pairs={{0,1},{1,0},{2,3},{3,2},{4,5},{5,4},{6,7},{7,6},{8,9},{9,8},{10,11... | collective-permute-start | bytes 2457608 | tf_op jit(solution)/shard_map/ppermute | solution.py:32
  74.2 18.2 %collective-permute-start.20 = (bf16[2,80,1280]{2,1,0:T(8,128)(2,1)S(1)}, bf16[2,80,1280]{2,1,0:T(8,128)(2,1)S(1)}, u32[]{:S(2)}, u32[]{:S(2)}) collective-permute-start(bf16[2,80,1280]{2,1,0:T(8,128)(2,1)S(1)} %slice.162), channel_id=1, source_target_pairs={{0,2},{1,3},{2,4},{3,5},{4,6},{5,7},{6,0},{7,1},{8,10},{9,11},{10,... | collective-permute-start | bytes 1228808 | tf_op jit(solution)/shard_map/ppermute | solution.py:32
  83.7 13.2 %collective-permute-start.21 = (bf16[2,80,1280]{2,1,0:T(8,128)(2,1)S(1)}, bf16[2,80,1280]{2,1,0:T(8,128)(2,1)S(1)}, u32[]{:S(2)}, u32[]{:S(2)}) collective-permute-start(bf16[2,80,1280]{2,1,0:T(8,128)(2,1)S(1)} %slice.163), channel_id=1, source_target_pairs={{0,6},{1,7},{2,0},{3,1},{4,2},{5,3},{6,4},{7,5},{8,14},{9,15},{10,... | collective-permute-start | bytes 1228808 | tf_op jit(solution)/shard_map/ppermute | solution.py:32
  86.9 14.0 %collective-permute-start.9 = (bf16[2,40,2560]{2,1,0:T(8,128)(2,1)S(1)}, bf16[2,40,2560]{2,1,0:T(8,128)(2,1)S(1)}, u32[]{:S(2)}, u32[]{:S(2)}) collective-permute-start(bf16[2,40,2560]{2,1,0:T(8,128)(2,1)S(1)} %slice.160), channel_id=1, source_target_pairs={{0,2},{1,3},{2,4},{3,5},{4,6},{5,7},{6,0},{7,1},{8,10},{9,11},{10,... | collective-permute-start | bytes 1228808 | tf_op jit(solution)/shard_map/ppermute | solution.py:32
  87.1 16.6 %collective-permute-start.10 = (bf16[2,40,2560]{2,1,0:T(8,128)(2,1)S(1)}, bf16[2,40,2560]{2,1,0:T(8,128)(2,1)S(1)}, u32[]{:S(2)}, u32[]{:S(2)}) collective-permute-start(bf16[2,40,2560]{2,1,0:T(8,128)(2,1)S(1)} %slice.161), channel_id=1, source_target_pairs={{0,6},{1,7},{2,0},{3,1},{4,2},{5,3},{6,4},{7,5},{8,14},{9,15},{10,... | collective-permute-start | bytes 1228808 | tf_op jit(solution)/shard_map/ppermute | solution.py:32
  89.4 14.5 %collective-permute-start.17 = (bf16[4,80,1280]{2,1,0:T(8,128)(2,1)S(1)}, bf16[4,80,1280]{2,1,0:T(8,128)(2,1)S(1)}, u32[]{:S(2)}, u32[]{:S(2)}) collective-permute-start(bf16[4,80,1280]{2,1,0:T(8,128)(2,1)S(1)} %collective-permute-done.16), channel_id=1, source_target_pairs={{0,1},{1,0},{2,3},{3,2},{4,5},{5,4},{6,7},{7,6},{8,9},{9,8},{10,11... | collective-permute-start | bytes 2457608 | tf_op jit(solution)/shard_map/ppermute | solution.py:32
  137.5 14.8 %collective-permute-start.27 = (bf16[4,2,8,512]{3,2,1,0:T(8,128)(2,1)S(1)}, bf16[4,2,8,512]{3,2,1,0:T(8,128)(2,1)S(1)}, u32[]{:S(2)}, u32[]{:S(2)}) collective-permute-start(bf16[4,2,8,512]{3,2,1,0:T(8,128)(2,1)S(1)} %constant_dynamic-slice_fusion.4), channel_id=1, source_target_pairs={{0,24},{1,25},{2,26},{3,27},{4,28},{5,29},{6,30},{7,31},{8,0},{9,1... | collective-permute-start | bytes 196616 | tf_op jit(solution)/shard_map/ppermute | solution.py:32
  146.2 237.5 %collective-permute-start.48 = (bf16[4,4,80,352]{3,2,1,0:T(8,128)(2,1)}, bf16[4,4,80,352]{3,2,1,0:T(8,128)(2,1)}, u32[]{:S(2)}, u32[]{:S(2)}) collective-permute-start(bf16[4,4,80,352]{3,2,1,0:T(8,128)(2,1)} %bitcast.310), channel_id=1, source_target_pairs={{0,1},{1,0},{2,3},{3,2},{4,5},{5,4},{6,7},{7,6},{8,9},{9,8},{10,11... | collective-permute-start | bytes 2703368 | tf_op jit(solution)/shard_map/ppermute | solution.py:32
  224.2 74.7 %collective-permute-start = (bf16[88,1280]{1,0:T(8,128)(2,1)S(1)}, bf16[88,1280]{1,0:T(8,128)(2,1)S(1)}, u32[]{:S(2)}, u32[]{:S(2)}) collective-permute-start(bf16[88,1280]{1,0:T(8,128)(2,1)S(1)} %get-tuple-element.522), channel_id=1, source_target_pairs={{32,0},{64,32},{96,64},{128,96},{160,128},{192,160},{224,192},{33,... | collective-permute-start | bytes 675848 | tf_op jit(solution)/shard_map/while/body/eval_jaxpr/ppermute | solution.py:151
  383.4 52.9 %collective-permute-start.38 = (bf16[352,2560]{1,0:T(8,128)(2,1)S(1)}, bf16[352,2560]{1,0:T(8,128)(2,1)S(1)}, u32[]{:S(2)}, u32[]{:S(2)}) collective-permute-start(bf16[352,2560]{1,0:T(8,128)(2,1)S(1)} %bitcast.338), channel_id=1, source_target_pairs={{0,1},{1,0},{2,3},{3,2},{4,5},{5,4},{6,7},{7,6},{8,9},{9,8},{10,11... | collective-permute-start | bytes 5406728 | tf_op jit(solution)/shard_map/ppermute | solution.py:32
  393.7 14.3 %collective-permute-start.54 = (bf16[2,80,1280]{2,1,0:T(8,128)(2,1)S(1)}, bf16[2,80,1280]{2,1,0:T(8,128)(2,1)S(1)}, u32[]{:S(2)}, u32[]{:S(2)}) collective-permute-start(bf16[2,80,1280]{2,1,0:T(8,128)(2,1)S(1)} %get-tuple-element.427), channel_id=1, source_target_pairs={{0,6},{1,7},{2,0},{3,1},{4,2},{5,3},{6,4},{7,5},{8,14},{9,15},{10,... | collective-permute-start | bytes 1228808 | tf_op jit(solution)/shard_map/ppermute | solution.py:32
  397.9 20.7 %collective-permute-start.53 = (bf16[2,80,1280]{2,1,0:T(8,128)(2,1)S(1)}, bf16[2,80,1280]{2,1,0:T(8,128)(2,1)S(1)}, u32[]{:S(2)}, u32[]{:S(2)}) collective-permute-start(bf16[2,80,1280]{2,1,0:T(8,128)(2,1)S(1)} %bitcast.349), channel_id=1, source_target_pairs={{0,2},{1,3},{2,4},{3,5},{4,6},{5,7},{6,0},{7,1},{8,10},{9,11},{10,... | collective-permute-start | bytes 1228808 | tf_op jit(solution)/shard_map/ppermute | solution.py:32
  398.1 20.0 %collective-permute-start.50 = (bf16[2,80,1280]{2,1,0:T(8,128)(2,1)S(1)}, bf16[2,80,1280]{2,1,0:T(8,128)(2,1)S(1)}, u32[]{:S(2)}, u32[]{:S(2)}) collective-permute-start(bf16[2,80,1280]{2,1,0:T(8,128)(2,1)S(1)} %get-tuple-element.428), channel_id=1, source_target_pairs={{0,2},{1,3},{2,4},{3,5},{4,6},{5,7},{6,0},{7,1},{8,10},{9,11},{10,... | collective-permute-start | bytes 1228808 | tf_op jit(solution)/shard_map/ppermute | solution.py:32
  400.0 25.2 %collective-permute-start.52 = (bf16[2,80,1280]{2,1,0:T(8,128)(2,1)S(1)}, bf16[2,80,1280]{2,1,0:T(8,128)(2,1)S(1)}, u32[]{:S(2)}, u32[]{:S(2)}) collective-permute-start(bf16[2,80,1280]{2,1,0:T(8,128)(2,1)S(1)} %bitcast.347), channel_id=1, source_target_pairs={{0,6},{1,7},{2,0},{3,1},{4,2},{5,3},{6,4},{7,5},{8,14},{9,15},{10,... | collective-permute-start | bytes 1228808 | tf_op jit(solution)/shard_map/ppermute | solution.py:32
  408.1 17.0 %collective-permute-start.55 = (bf16[2,80,1280]{2,1,0:T(8,128)(2,1)S(1)}, bf16[2,80,1280]{2,1,0:T(8,128)(2,1)S(1)}, u32[]{:S(2)}, u32[]{:S(2)}) collective-permute-start(bf16[2,80,1280]{2,1,0:T(8,128)(2,1)S(1)} %add_convert_fusion), channel_id=1, source_target_pairs={{0,6},{1,7},{2,0},{3,1},{4,2},{5,3},{6,4},{7,5},{8,14},{9,15},{10,... | collective-permute-start | bytes 1228808 | tf_op jit(solution)/shard_map/ppermute | solution.py:32
  429.1 54.9 %collective-permute-start.56 = (bf16[80,1280]{1,0:T(8,128)(2,1)S(1)}, bf16[80,1280]{1,0:T(8,128)(2,1)S(1)}, u32[]{:S(2)}, u32[]{:S(2)}) collective-permute-start(bf16[80,1280]{1,0:T(8,128)(2,1)S(1)} %get-tuple-element.424), channel_id=1, source_target_pairs={{0,8},{1,9},{2,10},{3,11},{4,12},{5,13},{6,14},{7,15},{8,16},{9,17... | collective-permute-start | bytes 614408 | tf_op jit(solution)/shard_map/ppermute | solution.py:32
  429.2 58.9 %collective-permute-start.57 = (bf16[80,1280]{1,0:T(8,128)(2,1)S(1)}, bf16[80,1280]{1,0:T(8,128)(2,1)S(1)}, u32[]{:S(2)}, u32[]{:S(2)}) collective-permute-start(bf16[80,1280]{1,0:T(8,128)(2,1)S(1)} %get-tuple-element.426), channel_id=1, source_target_pairs={{0,16},{1,17},{2,18},{3,19},{4,20},{5,21},{6,22},{7,23},{8,24},{9,... | collective-permute-start | bytes 614408 | tf_op jit(solution)/shard_map/ppermute | solution.py:32
  432.3 55.7 %collective-permute-start.58 = (bf16[80,1280]{1,0:T(8,128)(2,1)S(1)}, bf16[80,1280]{1,0:T(8,128)(2,1)S(1)}, u32[]{:S(2)}, u32[]{:S(2)}) collective-permute-start(bf16[80,1280]{1,0:T(8,128)(2,1)S(1)} %get-tuple-element.425), channel_id=1, source_target_pairs={{0,24},{1,25},{2,26},{3,27},{4,28},{5,29},{6,30},{7,31},{8,0},{9,1... | collective-permute-start | bytes 614408 | tf_op jit(solution)/shard_map/ppermute | solution.py:32
  442.6 19.0 %collective-permute-start.42 = (bf16[2,40,2560]{2,1,0:T(8,128)(2,1)S(1)}, bf16[2,40,2560]{2,1,0:T(8,128)(2,1)S(1)}, u32[]{:S(2)}, u32[]{:S(2)}) collective-permute-start(bf16[2,40,2560]{2,1,0:T(8,128)(2,1)S(1)} %bitcast.350), channel_id=1, source_target_pairs={{0,2},{1,3},{2,4},{3,5},{4,6},{5,7},{6,0},{7,1},{8,10},{9,11},{10,... | collective-permute-start | bytes 1228808 | tf_op jit(solution)/shard_map/ppermute | solution.py:32
  461.6 16.1 %collective-permute-start.41 = (bf16[2,40,2560]{2,1,0:T(8,128)(2,1)S(1)}, bf16[2,40,2560]{2,1,0:T(8,128)(2,1)S(1)}, u32[]{:S(2)}, u32[]{:S(2)}) collective-permute-start(bf16[2,40,2560]{2,1,0:T(8,128)(2,1)S(1)} %bitcast.348), channel_id=1, source_target_pairs={{0,6},{1,7},{2,0},{3,1},{4,2},{5,3},{6,4},{7,5},{8,14},{9,15},{10,... | collective-permute-start | bytes 1228808 | tf_op jit(solution)/shard_map/ppermute | solution.py:32
  480.7 13.4 %collective-permute-start.46 = (bf16[40,2560]{1,0:T(8,128)(2,1)S(1)}, bf16[40,2560]{1,0:T(8,128)(2,1)S(1)}, u32[]{:S(2)}, u32[]{:S(2)}) collective-permute-start(bf16[40,2560]{1,0:T(8,128)(2,1)S(1)} %get-tuple-element.431), channel_id=1, source_target_pairs={{0,16},{1,17},{2,18},{3,19},{4,20},{5,21},{6,22},{7,23},{8,24},{9,... | collective-permute-start | bytes 614408 | tf_op jit(solution)/shard_map/ppermute | solution.py:32
  484.0 14.2 %collective-permute-start.47 = (bf16[40,2560]{1,0:T(8,128)(2,1)S(1)}, bf16[40,2560]{1,0:T(8,128)(2,1)S(1)}, u32[]{:S(2)}, u32[]{:S(2)}) collective-permute-start(bf16[40,2560]{1,0:T(8,128)(2,1)S(1)} %get-tuple-element.430), channel_id=1, source_target_pairs={{0,24},{1,25},{2,26},{3,27},{4,28},{5,29},{6,30},{7,31},{8,0},{9,1... | collective-permute-start | bytes 614408 | tf_op jit(solution)/shard_map/ppermute | solution.py:32
  (62 other events, 602.4 us)
